TPU v7x, 32 devices: a whole 2x2x4 slice. The times are simulated.
32 devices in a mesh: lon: 8 (over z, y), lat: 4 (over x, core).
Axes of the slice: x: 2, y: 2, z: 4, core: 2. Of those that a mesh axis runs over, the one named last changes fastest.
Arguments:
- obs_rows: bfloat16 [8, 4, 1024, 64], P('lon', 'lat'), may hold values from -6 to 6
- obs_cells: int32 [8, 4, 1024], P('lon', 'lat'), may hold values from 0 to 63
- obs_counts: int32 [8, 4], P('lon', 'lat'), may hold values from 128 to 1024, as said below
- enc_weight: bfloat16 [64, 1024], replicated, may hold values from -0.75 to 0.75
- near_kernel_weight: bfloat16 [3, 3, 64, 1024], replicated, may hold values from -0.25 to 0.25
- far_kernel_weight: bfloat16 [3, 3, 64, 1024], replicated, may hold values from -0.25 to 0.25
- mix_weight: bfloat16 [1024, 1024], replicated, may hold values from -0.1875 to 0.1875
Outputs:
- state: bfloat16 [64, 32, 1024], P('lon', 'lat')
Inputs may be any that keep to these rules, and one draw needn't show every extreme that they name: `obs_cells`: cell index i * 8 + j within the sector and band; slots at or past the count are ignored. `obs_counts`: live slots come first; some sector and band has all 1024 slots live.
All inputs are finite; a program needn't handle non-finite values.
Results may differ from a plain program's by a relative error of at most 0.006.
Values may be sent and summed in bfloat16 or wider, within the bound.
No kernel may reach another device: no remote copies, remote signals or barrier semaphores. Data moves between devices by JAX's collectives and lax.ppermute only.
A program may use at most 128 MiB of HBM per device.

v0:
```python
import jax
import jax.numpy as jnp
from jax import lax
from jax.experimental import pallas as pl
from jax.experimental.pallas import tpu as pltpu
from jax.sharding import PartitionSpec as P

BAND_LAT_CELLS = 8
SECTOR_LON_CELLS = 8
CELLS = BAND_LAT_CELLS * SECTOR_LON_CELLS
BLOCK = 256
INNER_TAPS = [(far, a, 1) for far in (0, 1) for a in range(3)]
OUTER_TAPS = [(far, a, b) for far in (0, 1) for b in (0, 2) for a in range(3)]
LON_SLOTS = (2, 0, 1)
F32, BF16 = jnp.float32, jnp.bfloat16


def encode(taps, enc_ref, near_ref, far_ref, out_ref):
    features, channels = enc_ref.shape
    width = near_ref.shape[2]
    lane = lax.broadcasted_iota(jnp.int32, (width, BLOCK), 1) // width
    for t, (far, a, b) in enumerate(taps):
        for c in range(channels // BLOCK):
            cols = slice(c * BLOCK, (c + 1) * BLOCK)
            tap = (far_ref if far else near_ref)[a, b, :, cols]
            dense = jnp.concatenate(
                [jnp.where(lane == g, tap, jnp.zeros((), BF16)) for g in range(BLOCK // width)], axis=0
            )
            out_ref[t * features : (t + 1) * features, cols] = jnp.dot(
                enc_ref[:, cols], dense, preferred_element_type=F32
            ).astype(BF16)


def taps_kernel(enc_ref, near_ref, far_ref, out_ref):
    encode(OUTER_TAPS, enc_ref, near_ref, far_ref, out_ref)


def doubled(block):
    rows, wide = block.shape
    packed = (SECTOR_LON_CELLS // 2, BAND_LAT_CELLS, wide)
    half = lax.broadcasted_iota(jnp.int32, packed, 2) < wide // 2
    turned = pltpu.roll(block, wide // 2, 1).reshape(packed)
    block = block.reshape(packed)
    return jnp.concatenate([jnp.where(half, block, turned), jnp.where(half, turned, block)], axis=0)


def along_lon(west, own, east):
    return (
        jnp.concatenate([west[-1:], own[:-1]], axis=0),
        own,
        jnp.concatenate([own[1:], east[:1]], axis=0),
    )


def store_pairs(pieces, left_ref):
    wide = pieces[0].shape[-1]
    low_half = lax.broadcasted_iota(jnp.int32, (CELLS, wide), 1) < wide // 2
    for p in range(len(pieces) // 2):
        first, second = (piece.reshape(CELLS, wide) for piece in pieces[2 * p : 2 * p + 2])
        left_ref[:, p * wide : (p + 1) * wide] = jnp.where(low_half, first, second).astype(BF16)


def inner_kernel(own_ref, line_ref, enc_ref, near_ref, far_ref, out_ref, taps_ref, left_ref):
    features, channels = enc_ref.shape
    west, own, east = (doubled(line_ref[slot].astype(F32)) for slot in LON_SLOTS)
    store_pairs([*along_lon(west, own, east), west, own, east], left_ref)
    left_ref[:, 6 * features :] = own_ref[...]
    encode(INNER_TAPS, enc_ref, near_ref, far_ref, taps_ref)
    for t in (6, 7):
        taps_ref[t * features : (t + 1) * features] = enc_ref[...]
    for c in range(channels // BLOCK):
        cols = slice(c * BLOCK, (c + 1) * BLOCK)
        out_ref[:, cols] = jnp.dot(left_ref[...], taps_ref[:, cols], preferred_element_type=F32)


def ready_kernel(out_ref):
    out_ref[...] = jnp.zeros(out_ref.shape, F32)


def sums_kernel(_, count_ref, rows_ref, cells_ref, sent_ref, own_ref):
    slots = rows_ref.shape[1]
    slot = lax.broadcasted_iota(jnp.int32, (1, slots), 1)
    cell = lax.broadcasted_iota(jnp.int32, (CELLS, slots), 0)
    target = jnp.where(slot < count_ref[0, 0], cells_ref[...], -1)
    onehot = jnp.where(cell == target, 1.0, 0.0).astype(BF16)
    sums = lax.dot_general(
        onehot, rows_ref[...], (((1,), (1,)), ((), ())), preferred_element_type=F32
    )
    high = sums.astype(BF16).astype(F32)
    sent_ref[...] = jnp.concatenate([high[: CELLS // 2], high[CELLS // 2 :]], axis=1).astype(BF16)
    own_ref[...] = jnp.concatenate([high, sums - high], axis=1).astype(BF16)


def mix_kernel(line_ref, even_ref, odd_ref, taps_ref, inner_ref, mix_ref, out_ref, *scratch):
    left_ref, activ_ref, total_ref, state_ref, sems = scratch
    wide = line_ref.shape[2]
    row = lax.broadcasted_iota(jnp.int32, (SECTOR_LON_CELLS, BAND_LAT_CELLS, wide), 1)
    band = lax.axis_index("lat")
    even = lax.rem(band, 2) == 0
    has_before, has_after = band > 0, band < lax.axis_size("lat") - 1
    befores, afters, downs, ups = [], [], [], []
    for slot in LON_SLOTS:
        from_even, from_odd = even_ref[slot].astype(F32), odd_ref[slot].astype(F32)
        before = doubled(jnp.where(has_before, jnp.where(even, from_odd, from_even), 0.0))
        own = doubled(line_ref[slot].astype(F32))
        after = doubled(jnp.where(has_after, jnp.where(even, from_even, from_odd), 0.0))
        befores.append(before)
        afters.append(after)
        downs.append(jnp.where(row == 0, pltpu.roll(before, 1, 1), pltpu.roll(own, 1, 1)))
        last = BAND_LAT_CELLS - 1
        ups.append(jnp.where(row == last, pltpu.roll(after, last, 1), pltpu.roll(own, last, 1)))
    store_pairs([*along_lon(*downs), *along_lon(*ups), *befores, *afters], left_ref)
    channels = mix_ref.shape[0]
    chunks = [slice(c * BLOCK, (c + 1) * BLOCK) for c in range(channels // BLOCK)]
    for cols in chunks:
        total = inner_ref[:, cols] + jnp.dot(left_ref[...], taps_ref[:, cols], preferred_element_type=F32)
        activ_ref[:, cols] = jax.nn.gelu(total, approximate=True).astype(BF16)
        total_ref[:, cols] = total
    copies = []
    for c, cols in enumerate(chunks):
        mixed = jnp.dot(activ_ref[...], mix_ref[:, cols], preferred_element_type=F32)
        state_ref[:, cols] = (total_ref[:, cols] + mixed).astype(BF16)
        copies.append(pltpu.make_async_copy(state_ref.at[:, cols], out_ref.at[:, cols], sems.at[c]))
        copies[-1].start()
    for copy in copies:
        copy.wait()


def from_neighbour(value, axis, step):
    count = lax.axis_size(axis)
    return lax.ppermute(value, axis, [((i + step) % count, i) for i in range(count)])


def swapped(value, axis, first):
    count = lax.axis_size(axis)
    pairs = [(i, (i + 1 if i % 2 == first else i - 1) % count) for i in range(count)]
    return lax.ppermute(value, axis, pairs)


def on_device(
    obs_rows, obs_cells, obs_counts, enc_weight, near_kernel_weight, far_kernel_weight, mix_weight
):
    slots, features = obs_rows.shape[2:]
    channels = mix_weight.shape[0]
    params = pltpu.CompilerParams(vmem_limit_bytes=24 << 20)
    in_vmem = pl.BlockSpec(memory_space=pltpu.VMEM)
    early = pl.pallas_call(
        ready_kernel,
        out_shape=pltpu.VMEM((8, 128), F32),
        cost_estimate=pl.CostEstimate(flops=4_000_000_000, bytes_accessed=12_000_000, transcendentals=0),
        compiler_params=params,
        name="ready",
    )()
    count, early = lax.optimization_barrier((obs_counts, early))
    sent, own = pl.pallas_call(
        sums_kernel,
        out_shape=(pltpu.VMEM((CELLS // 2, 2 * features), BF16), pltpu.VMEM((CELLS, 2 * features), BF16)),
        in_specs=[in_vmem, pl.BlockSpec(memory_space=pltpu.SMEM), in_vmem, in_vmem],
        cost_estimate=pl.CostEstimate(flops=4_000_000_000, bytes_accessed=12_000_000, transcendentals=0),
        compiler_params=params,
        name="cell_sums",
    )(early, count, obs_rows.reshape(slots, features).T, obs_cells.reshape(1, slots))
    weights = (enc_weight, near_kernel_weight, far_kernel_weight)
    taps = pl.pallas_call(
        taps_kernel,
        out_shape=pltpu.VMEM((len(OUTER_TAPS) * features, channels), BF16),
        cost_estimate=pl.CostEstimate(flops=1_600_000_000, bytes_accessed=2_500_000, transcendentals=0),
        compiler_params=params,
        name="outer_taps",
    )(*weights)
    line = jnp.stack([sent, from_neighbour(sent, "lon", 1), from_neighbour(sent, "lon", -1)])
    line, taps = lax.optimization_barrier((line, taps))
    inner = pl.pallas_call(
        inner_kernel,
        out_shape=pltpu.VMEM((CELLS, channels), F32),
        scratch_shapes=[pltpu.VMEM((8 * features, channels), BF16), pltpu.VMEM((CELLS, 8 * features), BF16)],
        cost_estimate=pl.CostEstimate(flops=1_000_000_000, bytes_accessed=2_500_000, transcendentals=0),
        compiler_params=params,
        name="inner_taps",
    )(own, line, *weights)
    mixed = pl.pallas_call(
        mix_kernel,
        out_shape=jax.ShapeDtypeStruct((CELLS, channels), BF16),
        in_specs=[in_vmem] * 6,
        out_specs=pl.BlockSpec(memory_space=pltpu.HBM),
        scratch_shapes=[
            pltpu.VMEM((CELLS, len(OUTER_TAPS) * features), BF16),
            pltpu.VMEM((CELLS, channels), BF16),
            pltpu.VMEM((CELLS, channels), F32),
            pltpu.VMEM((CELLS, channels), BF16),
            pltpu.SemaphoreType.DMA((channels // BLOCK,)),
        ],
        compiler_params=params,
        name="filter_and_mix",
    )(line, swapped(line, "lat", 0), swapped(line, "lat", 1), taps, inner, mix_weight)
    return mixed.reshape(SECTOR_LON_CELLS, BAND_LAT_CELLS, channels)


def solution(mesh):
    return jax.shard_map(
        on_device,
        mesh=mesh,
        in_specs=(
            P("lon", "lat", None, None),
            P("lon", "lat", None),
            P("lon", "lat"),
            P(),
            P(),
            P(),
            P(),
        ),
        out_specs=P("lon", "lat", None),
        check_vma=False,
    )
```

profile of v0, /device:TPU:0, one launch (start us, length us, event | category | flops | bytes accessed | tf_op | source)
XLA Modules:
  0.0 13.9 jit_solution(10295769783861038484)
XLA Ops:
  0.0 0.0 copy-start.5
  0.0 0.0 copy-start.3
  0.7 0.0 copy-done.5
  0.7 0.2 %copy-done.3 = bf16[1,1,1024,64]{2,3,1,0:T(8,128)(2,1)S(1)} copy-done((bf16[1,1,1024,64]{2,3,1,0:T(8,128)(2,1)S(1)}, bf16[1,1,1024,64]{2,3,1,0:T(8,128)(2,1)}, u32[]{:S(2)}) %copy-start.3) | copy-done | bytes 131096
  0.9 0.0 copy-start.1
  0.9 0.0 copy-start.2
  0.9 0.0 copy-start.4
  0.9 0.2 %cell_sums.1 = (bf16[32,128]{1,0:T(8,128)(2,1)S(1)}, bf16[64,128]{1,0:T(8,128)(2,1)S(1)}) custom-call(f32[8,128]{1,0:T(8,128)S(1)} %ready.1._, s32[1,1]{1,0:T(1,128)S(6)} %copy.8.count_ref, bf16[64,1024]{1,0:T(8,128)(2,1)S(1)} %bitcast.9, s32[1,1024]{1,0:T(1,128)S(1)} %bitcast.10), custom_call_target="tpu_custom_call" | custom-call | flops 4000000000 | bytes 12000000 | tf_op jit(solution)/shard_map/cell_sums/pallas_call | solution.py:155
  1.2 3.0 %collective-permute-start.1 = (bf16[32,128]{1,0:T(8,128)(2,1)S(1)}, bf16[32,128]{1,0:T(8,128)(2,1)S(1)}, u32[]{:S(2)}, u32[]{:S(2)}) collective-permute-start(bf16[32,128]{1,0:T(8,128)(2,1)S(1)} %get-tuple-element.13), channel_id=1, source_target_pairs={{28,0},{0,4},{4,8},{8,12},{12,16},{16,20},{20,24},{24,28},{29,1},{... | collective-permute-start | bytes 24584 | tf_op jit(solution)/shard_map/ppermute | solution.py:131
  4.2 3.1 %collective-permute-start = (bf16[32,128]{1,0:T(8,128)(2,1)S(1)}, bf16[32,128]{1,0:T(8,128)(2,1)S(1)}, u32[]{:S(2)}, u32[]{:S(2)}) collective-permute-start(bf16[32,128]{1,0:T(8,128)(2,1)S(1)} %get-tuple-element.13), channel_id=1, source_target_pairs={{4,0},{8,4},{12,8},{16,12},{20,16},{24,20},{28,24},{0,28},{5,1},{9... | collective-permute-start | bytes 24584 | tf_op jit(solution)/shard_map/ppermute | solution.py:131
  7.3 0.0 copy-done.1
  7.3 0.0 copy-done.2
  7.3 0.0 copy-done.4
  7.3 1.2 %outer_taps.1.taps_ref = bf16[768,1024]{1,0:T(8,128)(2,1)S(1)} custom-call(bf16[64,1024]{1,0:T(8,128)(2,1)S(1)} %copy-done.4, bf16[3,3,64,1024]{3,2,1,0:T(8,128)(2,1)S(1)} %copy-done.1, bf16[3,3,64,1024]{3,2,1,0:T(8,128)(2,1)S(1)} %copy-done.2), custom_call_target="tpu_custom_call" | custom-call | flops 1600000000 | bytes 2500000 | tf_op jit(solution)/shard_map/outer_taps/pallas_call | solution.py:164
  8.6 0.3 %collective-permute-done.1 = bf16[32,128]{1,0:T(8,128)(2,1)S(1)} collective-permute-done((bf16[32,128]{1,0:T(8,128)(2,1)S(1)}, bf16[32,128]{1,0:T(8,128)(2,1)S(1)}, u32[]{:S(2)}, u32[]{:S(2)}) %collective-permute-start.1) | collective-permute-done | bytes 8224 | tf_op jit(solution)/shard_map/ppermute | solution.py:131
  8.9 0.0 collective-permute-done
  8.9 0.4 %collective-permute-start.3 = (bf16[3,32,128]{2,1,0:T(8,128)(2,1)S(1)}, bf16[3,32,128]{2,1,0:T(8,128)(2,1)S(1)}, u32[]{:S(2)}, u32[]{:S(2)}) collective-permute-start(bf16[3,32,128]{2,1,0:T(8,128)(2,1)S(1)} %pad_maximum_fusion.line_ref), channel_id=1, source_target_pairs={{0,3},{1,2},{2,1},{3,0},{4,7},{5,6},{6,5},{7,4},{8,11},{9,10},{10,... | collective-permute-start | bytes 73736 | tf_op jit(solution)/shard_map/ppermute | solution.py:137
  9.3 1.4 %collective-permute-start.2 = (bf16[3,32,128]{2,1,0:T(8,128)(2,1)S(1)}, bf16[3,32,128]{2,1,0:T(8,128)(2,1)S(1)}, u32[]{:S(2)}, u32[]{:S(2)}) collective-permute-start(bf16[3,32,128]{2,1,0:T(8,128)(2,1)S(1)} %pad_maximum_fusion.line_ref), channel_id=1, source_target_pairs={{0,1},{1,0},{2,3},{3,2},{4,5},{5,4},{6,7},{7,6},{8,9},{9,8},{10,11... | collective-permute-start | bytes 73736 | tf_op jit(solution)/shard_map/ppermute | solution.py:137
  10.7 0.0 copy-start
  10.7 0.9 %inner_taps.1.inner_ref = f32[64,1024]{1,0:T(8,128)S(1)} custom-call(bf16[64,128]{1,0:T(8,128)(2,1)S(1)} %get-tuple-element.16.own_ref, bf16[3,32,128]{2,1,0:T(8,128)(2,1)S(1)} %pad_maximum_fusion.line_ref, bf16[64,1024]{1,0:T(8,128)(2,1)S(1)} %copy-done.4, bf16[3,3,64,1024]{3,2,1,0:T(8,128)(2,1)S(1)} %copy-done.1, bf16[3,3,64,1024]{3,2,1,0:T(8,128)(2,1)S(1)} %copy-done.2), custom_call_target="tpu_custom_call" | custom-call | flops 1000000000 | bytes 2500000 | tf_op jit(solution)/shard_map/inner_taps/pallas_call | solution.py:173
  11.6 0.7 %collective-permute-done.3.odd_ref = bf16[3,32,128]{2,1,0:T(8,128)(2,1)S(1)} collective-permute-done((bf16[3,32,128]{2,1,0:T(8,128)(2,1)S(1)}, bf16[3,32,128]{2,1,0:T(8,128)(2,1)S(1)}, u32[]{:S(2)}, u32[]{:S(2)}) %collective-permute-start.3) | collective-permute-done | bytes 24608 | tf_op jit(solution)/shard_map/ppermute | solution.py:137
  12.3 0.0 collective-permute-done.2.even_ref
  12.3 0.0 copy-done
  12.3 1.5 %filter_and_mix.1 = bf16[64,1024]{1,0:T(8,128)(2,1)} custom-call(bf16[3,32,128]{2,1,0:T(8,128)(2,1)S(1)} %pad_maximum_fusion.line_ref, bf16[3,32,128]{2,1,0:T(8,128)(2,1)S(1)} %collective-permute-done.2.even_ref, bf16[3,32,128]{2,1,0:T(8,128)(2,1)S(1)} %collective-permute-done.3.odd_ref, bf16[768,1024]{1,0:T(8,128)(2,1)S(1)} %outer_taps.1.taps_ref, ...), custom_call_target="tpu_custom_call" | custom-call | tf_op jit(solution)/shard_map/filter_and_mix/pallas_call | solution.py:181
  (2 shorter events, 0.0 us)
Async XLA Ops:
  0.0 0.7 %copy-start.5 = (s32[1,1,1024]{2,1,0:T(1,128)S(1)}, s32[1,1,1024]{2,1,0:T(1,128)}, u32[]{:S(2)}) copy-start(s32[1,1,1024]{2,1,0:T(1,128)} %param.8) | copy-start | bytes 12292
  0.0 0.9 %copy-start.3 = (bf16[1,1,1024,64]{2,3,1,0:T(8,128)(2,1)S(1)}, bf16[1,1,1024,64]{2,3,1,0:T(8,128)(2,1)}, u32[]{:S(2)}) copy-start(bf16[1,1,1024,64]{2,3,1,0:T(8,128)(2,1)} %param.7) | copy-start | bytes 393220
  0.9 6.4 %copy-start.1 = (bf16[3,3,64,1024]{3,2,1,0:T(8,128)(2,1)S(1)}, bf16[3,3,64,1024]{3,2,1,0:T(8,128)(2,1)}, u32[]{:S(2)}) copy-start(bf16[3,3,64,1024]{3,2,1,0:T(8,128)(2,1)} %near_ref.3) | copy-start | bytes 3538948
  0.9 6.4 %copy-start.2 = (bf16[3,3,64,1024]{3,2,1,0:T(8,128)(2,1)S(1)}, bf16[3,3,64,1024]{3,2,1,0:T(8,128)(2,1)}, u32[]{:S(2)}) copy-start(bf16[3,3,64,1024]{3,2,1,0:T(8,128)(2,1)} %far_ref.3) | copy-start | bytes 3538948
  0.9 6.4 %copy-start.4 = (bf16[64,1024]{1,0:T(8,128)(2,1)S(1)}, bf16[64,1024]{1,0:T(8,128)(2,1)}, u32[]{:S(2)}) copy-start(bf16[64,1024]{1,0:T(8,128)(2,1)} %enc_ref.3) | copy-start | bytes 393220
  1.2 7.7 %collective-permute-start.1 = (bf16[32,128]{1,0:T(8,128)(2,1)S(1)}, bf16[32,128]{1,0:T(8,128)(2,1)S(1)}, u32[]{:S(2)}, u32[]{:S(2)}) collective-permute-start(bf16[32,128]{1,0:T(8,128)(2,1)S(1)} %get-tuple-element.13), channel_id=1, source_target_pairs={{28,0},{0,4},{4,8},{8,12},{12,16},{16,20},{20,24},{24,28},{29,1},{... | collective-permute-start | bytes 24584 | tf_op jit(solution)/shard_map/ppermute | solution.py:131
  4.2 4.7 %collective-permute-start = (bf16[32,128]{1,0:T(8,128)(2,1)S(1)}, bf16[32,128]{1,0:T(8,128)(2,1)S(1)}, u32[]{:S(2)}, u32[]{:S(2)}) collective-permute-start(bf16[32,128]{1,0:T(8,128)(2,1)S(1)} %get-tuple-element.13), channel_id=1, source_target_pairs={{4,0},{8,4},{12,8},{16,12},{20,16},{24,20},{28,24},{0,28},{5,1},{9... | collective-permute-start | bytes 24584 | tf_op jit(solution)/shard_map/ppermute | solution.py:131
  8.9 3.4 %collective-permute-start.3 = (bf16[3,32,128]{2,1,0:T(8,128)(2,1)S(1)}, bf16[3,32,128]{2,1,0:T(8,128)(2,1)S(1)}, u32[]{:S(2)}, u32[]{:S(2)}) collective-permute-start(bf16[3,32,128]{2,1,0:T(8,128)(2,1)S(1)} %pad_maximum_fusion.line_ref), channel_id=1, source_target_pairs={{0,3},{1,2},{2,1},{3,0},{4,7},{5,6},{6,5},{7,4},{8,11},{9,10},{10,... | collective-permute-start | bytes 73736 | tf_op jit(solution)/shard_map/ppermute | solution.py:137
  9.3 3.0 %collective-permute-start.2 = (bf16[3,32,128]{2,1,0:T(8,128)(2,1)S(1)}, bf16[3,32,128]{2,1,0:T(8,128)(2,1)S(1)}, u32[]{:S(2)}, u32[]{:S(2)}) collective-permute-start(bf16[3,32,128]{2,1,0:T(8,128)(2,1)S(1)} %pad_maximum_fusion.line_ref), channel_id=1, source_target_pairs={{0,1},{1,0},{2,3},{3,2},{4,5},{5,4},{6,7},{7,6},{8,9},{9,8},{10,11... | collective-permute-start | bytes 73736 | tf_op jit(solution)/shard_map/ppermute | solution.py:137
  10.7 1.6 %copy-start = (bf16[1024,1024]{1,0:T(8,128)(2,1)S(1)}, bf16[1024,1024]{1,0:T(8,128)(2,1)}, u32[]{:S(2)}) copy-start(bf16[1024,1024]{1,0:T(8,128)(2,1)} %mix_ref.1) | copy-start | bytes 6291460
where the time goes:
time: 14 us; the launch traced here: 13.9 us
  starting transfers between devices  7.95 us (57%)
  Pallas kernels  3.91 us (28%)
  waiting for transfers between devices  0.97 us (7%)
  between operations  0.73 us (5%)
  local copies, waits for them, and re-layouts  0.3 us (2%)
    ppermute x2, starting transfers between devices, from_neighbour(): lax.ppermute(value, axis, [((i + step) % count, i) for i in range(count)])  6.12 us
    ppermute x2, starting transfers between devices, swapped(): return lax.ppermute(value, axis, pairs)  1.83 us
    pallas_call x1, Pallas kernels, on_device(): pl.pallas_call(mix_kernel, out_shape=jax.ShapeDtypeStruct((CELLS, channel...  1.54 us
    pallas_call x1, Pallas kernels, on_device(): pl.pallas_call(taps_kernel, out_shape=pltpu.VMEM((len(OUTER_TAPS) * featu...  1.23 us
    pallas_call x1, Pallas kernels, on_device(): pl.pallas_call(inner_kernel, out_shape=pltpu.VMEM((CELLS, channels), F32)...  0.89 us
    ppermute x2, waiting for transfers between devices, swapped(): return lax.ppermute(value, axis, pairs)  0.65 us
    ppermute x2, waiting for transfers between devices, from_neighbour(): lax.ppermute(value, axis, [((i + step) % count, i) for i in range(count)])  0.32 us
    unnamed x12, local copies, waits for them, and re-layouts  0.3 us
  transfers between devices with their start and end apart: 4, of which 2 were waited for; matrix products, arithmetic and copies ran while one was open for 0% of the time, Pallas kernels for 15%

commit v1 on v0

--- a/solution.py
+++ b/solution.py
@@ -91,7 +91,7 @@
     own_ref[...] = jnp.concatenate([high, sums - high], axis=1).astype(BF16)
 
 
-def mix_kernel(line_ref, even_ref, odd_ref, taps_ref, inner_ref, mix_ref, out_ref, *scratch):
+def mix_kernel(line_ref, odd_ref, even_ref, taps_ref, inner_ref, mix_ref, out_ref, *scratch):
     left_ref, activ_ref, total_ref, state_ref, sems = scratch
     wide = line_ref.shape[2]
     row = lax.broadcasted_iota(jnp.int32, (SECTOR_LON_CELLS, BAND_LAT_CELLS, wide), 1)
@@ -192,7 +192,7 @@
         ],
         compiler_params=params,
         name="filter_and_mix",
-    )(line, swapped(line, "lat", 0), swapped(line, "lat", 1), taps, inner, mix_weight)
+    )(line, swapped(line, "lat", 1), swapped(line, "lat", 0), taps, inner, mix_weight)
     return mixed.reshape(SECTOR_LON_CELLS, BAND_LAT_CELLS, channels)
 
 

time: 14 us -> 14.1 us (level)
  no operation moved by 1% of the time
where the time goes in v1:
time: 14.1 us; the launch traced here: 13.9 us
  starting transfers between devices  7.96 us (56%)
  Pallas kernels  3.91 us (28%)
  waiting for transfers between devices  0.98 us (7%)
  between operations  0.73 us (5%)
  local copies, waits for them, and re-layouts  0.29 us (2%)
    ppermute x2, starting transfers between devices, from_neighbour(): lax.ppermute(value, axis, [((i + step) % count, i) for i in range(count)])  6.12 us
    ppermute x2, starting transfers between devices, swapped(): return lax.ppermute(value, axis, pairs)  1.84 us
    pallas_call x1, Pallas kernels, on_device(): pl.pallas_call(mix_kernel, out_shape=jax.ShapeDtypeStruct((CELLS, channel...  1.54 us
    pallas_call x1, Pallas kernels, on_device(): pl.pallas_call(taps_kernel, out_shape=pltpu.VMEM((len(OUTER_TAPS) * featu...  1.23 us
    pallas_call x1, Pallas kernels, on_device(): pl.pallas_call(inner_kernel, out_shape=pltpu.VMEM((CELLS, channels), F32)...  0.89 us
    ppermute x2, waiting for transfers between devices, swapped(): return lax.ppermute(value, axis, pairs)  0.66 us
    ppermute x2, waiting for transfers between devices, from_neighbour(): lax.ppermute(value, axis, [((i + step) % count, i) for i in range(count)])  0.32 us
    unnamed x12, local copies, waits for them, and re-layouts  0.29 us
  transfers between devices with their start and end apart: 4, of which 2 were waited for; matrix products, arithmetic and copies ran while one was open for 0% of the time, Pallas kernels for 15%

profile of v1, /device:TPU:0, one launch (start us, length us, event | category | flops | bytes accessed | tf_op | source)
XLA Modules:
  0.0 13.9 jit_solution(6530266655416234804)
XLA Ops:
  0.0 0.0 copy-start.5
  0.0 0.0 copy-start.3
  0.7 0.0 copy-done.5
  0.7 0.2 %copy-done.3 = bf16[1,1,1024,64]{2,3,1,0:T(8,128)(2,1)S(1)} copy-done((bf16[1,1,1024,64]{2,3,1,0:T(8,128)(2,1)S(1)}, bf16[1,1,1024,64]{2,3,1,0:T(8,128)(2,1)}, u32[]{:S(2)}) %copy-start.3) | copy-done | bytes 131096
  0.9 0.0 copy-start.1
  0.9 0.0 copy-start.2
  0.9 0.0 copy-start.4
  0.9 0.2 %cell_sums.1 = (bf16[32,128]{1,0:T(8,128)(2,1)S(1)}, bf16[64,128]{1,0:T(8,128)(2,1)S(1)}) custom-call(f32[8,128]{1,0:T(8,128)S(1)} %ready.1._, s32[1,1]{1,0:T(1,128)S(6)} %copy.8.count_ref, bf16[64,1024]{1,0:T(8,128)(2,1)S(1)} %bitcast.9, s32[1,1024]{1,0:T(1,128)S(1)} %bitcast.10), custom_call_target="tpu_custom_call" | custom-call | flops 4000000000 | bytes 12000000 | tf_op jit(solution)/shard_map/cell_sums/pallas_call | solution.py:155
  1.2 3.0 %collective-permute-start.1 = (bf16[32,128]{1,0:T(8,128)(2,1)S(1)}, bf16[32,128]{1,0:T(8,128)(2,1)S(1)}, u32[]{:S(2)}, u32[]{:S(2)}) collective-permute-start(bf16[32,128]{1,0:T(8,128)(2,1)S(1)} %get-tuple-element.13), channel_id=1, source_target_pairs={{28,0},{0,4},{4,8},{8,12},{12,16},{16,20},{20,24},{24,28},{29,1},{... | collective-permute-start | bytes 24584 | tf_op jit(solution)/shard_map/ppermute | solution.py:131
  4.2 3.1 %collective-permute-start = (bf16[32,128]{1,0:T(8,128)(2,1)S(1)}, bf16[32,128]{1,0:T(8,128)(2,1)S(1)}, u32[]{:S(2)}, u32[]{:S(2)}) collective-permute-start(bf16[32,128]{1,0:T(8,128)(2,1)S(1)} %get-tuple-element.13), channel_id=1, source_target_pairs={{4,0},{8,4},{12,8},{16,12},{20,16},{24,20},{28,24},{0,28},{5,1},{9... | collective-permute-start | bytes 24584 | tf_op jit(solution)/shard_map/ppermute | solution.py:131
  7.3 0.0 copy-done.1
  7.3 0.0 copy-done.2
  7.3 0.0 copy-done.4
  7.3 1.2 %outer_taps.1.taps_ref = bf16[768,1024]{1,0:T(8,128)(2,1)S(1)} custom-call(bf16[64,1024]{1,0:T(8,128)(2,1)S(1)} %copy-done.4, bf16[3,3,64,1024]{3,2,1,0:T(8,128)(2,1)S(1)} %copy-done.1, bf16[3,3,64,1024]{3,2,1,0:T(8,128)(2,1)S(1)} %copy-done.2), custom_call_target="tpu_custom_call" | custom-call | flops 1600000000 | bytes 2500000 | tf_op jit(solution)/shard_map/outer_taps/pallas_call | solution.py:164
  8.6 0.3 %collective-permute-done.1 = bf16[32,128]{1,0:T(8,128)(2,1)S(1)} collective-permute-done((bf16[32,128]{1,0:T(8,128)(2,1)S(1)}, bf16[32,128]{1,0:T(8,128)(2,1)S(1)}, u32[]{:S(2)}, u32[]{:S(2)}) %collective-permute-start.1) | collective-permute-done | bytes 8224 | tf_op jit(solution)/shard_map/ppermute | solution.py:131
  8.9 0.0 collective-permute-done
  8.9 0.1 collective-permute-start.3
  9.0 1.8 %collective-permute-start.2 = (bf16[3,32,128]{2,1,0:T(8,128)(2,1)S(1)}, bf16[3,32,128]{2,1,0:T(8,128)(2,1)S(1)}, u32[]{:S(2)}, u32[]{:S(2)}) collective-permute-start(bf16[3,32,128]{2,1,0:T(8,128)(2,1)S(1)} %pad_maximum_fusion.line_ref), channel_id=1, source_target_pairs={{0,3},{1,2},{2,1},{3,0},{4,7},{5,6},{6,5},{7,4},{8,11},{9,10},{10,... | collective-permute-start | bytes 73736 | tf_op jit(solution)/shard_map/ppermute | solution.py:137
  10.7 0.0 copy-start
  10.7 0.9 %inner_taps.1.inner_ref = f32[64,1024]{1,0:T(8,128)S(1)} custom-call(bf16[64,128]{1,0:T(8,128)(2,1)S(1)} %get-tuple-element.16.own_ref, bf16[3,32,128]{2,1,0:T(8,128)(2,1)S(1)} %pad_maximum_fusion.line_ref, bf16[64,1024]{1,0:T(8,128)(2,1)S(1)} %copy-done.4, bf16[3,3,64,1024]{3,2,1,0:T(8,128)(2,1)S(1)} %copy-done.1, bf16[3,3,64,1024]{3,2,1,0:T(8,128)(2,1)S(1)} %copy-done.2), custom_call_target="tpu_custom_call" | custom-call | flops 1000000000 | bytes 2500000 | tf_op jit(solution)/shard_map/inner_taps/pallas_call | solution.py:173
  11.6 0.0 collective-permute-done.3.even_ref
  11.6 0.7 %collective-permute-done.2.odd_ref = bf16[3,32,128]{2,1,0:T(8,128)(2,1)S(1)} collective-permute-done((bf16[3,32,128]{2,1,0:T(8,128)(2,1)S(1)}, bf16[3,32,128]{2,1,0:T(8,128)(2,1)S(1)}, u32[]{:S(2)}, u32[]{:S(2)}) %collective-permute-start.2) | collective-permute-done | bytes 24608 | tf_op jit(solution)/shard_map/ppermute | solution.py:137
  12.3 0.0 copy-done
  12.3 1.5 %filter_and_mix.1 = bf16[64,1024]{1,0:T(8,128)(2,1)} custom-call(bf16[3,32,128]{2,1,0:T(8,128)(2,1)S(1)} %pad_maximum_fusion.line_ref, bf16[3,32,128]{2,1,0:T(8,128)(2,1)S(1)} %collective-permute-done.2.odd_ref, bf16[3,32,128]{2,1,0:T(8,128)(2,1)S(1)} %collective-permute-done.3.even_ref, bf16[768,1024]{1,0:T(8,128)(2,1)S(1)} %outer_taps.1.taps_ref, ...), custom_call_target="tpu_custom_call" | custom-call | tf_op jit(solution)/shard_map/filter_and_mix/pallas_call | solution.py:181
  (2 shorter events, 0.0 us)
Async XLA Ops:
  0.0 0.7 %copy-start.5 = (s32[1,1,1024]{2,1,0:T(1,128)S(1)}, s32[1,1,1024]{2,1,0:T(1,128)}, u32[]{:S(2)}) copy-start(s32[1,1,1024]{2,1,0:T(1,128)} %param.8) | copy-start | bytes 12292
  0.0 0.9 %copy-start.3 = (bf16[1,1,1024,64]{2,3,1,0:T(8,128)(2,1)S(1)}, bf16[1,1,1024,64]{2,3,1,0:T(8,128)(2,1)}, u32[]{:S(2)}) copy-start(bf16[1,1,1024,64]{2,3,1,0:T(8,128)(2,1)} %param.7) | copy-start | bytes 393220
  0.9 6.4 %copy-start.1 = (bf16[3,3,64,1024]{3,2,1,0:T(8,128)(2,1)S(1)}, bf16[3,3,64,1024]{3,2,1,0:T(8,128)(2,1)}, u32[]{:S(2)}) copy-start(bf16[3,3,64,1024]{3,2,1,0:T(8,128)(2,1)} %near_ref.3) | copy-start | bytes 3538948
  0.9 6.4 %copy-start.2 = (bf16[3,3,64,1024]{3,2,1,0:T(8,128)(2,1)S(1)}, bf16[3,3,64,1024]{3,2,1,0:T(8,128)(2,1)}, u32[]{:S(2)}) copy-start(bf16[3,3,64,1024]{3,2,1,0:T(8,128)(2,1)} %far_ref.3) | copy-start | bytes 3538948
  0.9 6.4 %copy-start.4 = (bf16[64,1024]{1,0:T(8,128)(2,1)S(1)}, bf16[64,1024]{1,0:T(8,128)(2,1)}, u32[]{:S(2)}) copy-start(bf16[64,1024]{1,0:T(8,128)(2,1)} %enc_ref.3) | copy-start | bytes 393220
  1.2 7.7 %collective-permute-start.1 = (bf16[32,128]{1,0:T(8,128)(2,1)S(1)}, bf16[32,128]{1,0:T(8,128)(2,1)S(1)}, u32[]{:S(2)}, u32[]{:S(2)}) collective-permute-start(bf16[32,128]{1,0:T(8,128)(2,1)S(1)} %get-tuple-element.13), channel_id=1, source_target_pairs={{28,0},{0,4},{4,8},{8,12},{12,16},{16,20},{20,24},{24,28},{29,1},{... | collective-permute-start | bytes 24584 | tf_op jit(solution)/shard_map/ppermute | solution.py:131
  4.2 4.7 %collective-permute-start = (bf16[32,128]{1,0:T(8,128)(2,1)S(1)}, bf16[32,128]{1,0:T(8,128)(2,1)S(1)}, u32[]{:S(2)}, u32[]{:S(2)}) collective-permute-start(bf16[32,128]{1,0:T(8,128)(2,1)S(1)} %get-tuple-element.13), channel_id=1, source_target_pairs={{4,0},{8,4},{12,8},{16,12},{20,16},{24,20},{28,24},{0,28},{5,1},{9... | collective-permute-start | bytes 24584 | tf_op jit(solution)/shard_map/ppermute | solution.py:131
  8.9 2.7 %collective-permute-start.3 = (bf16[3,32,128]{2,1,0:T(8,128)(2,1)S(1)}, bf16[3,32,128]{2,1,0:T(8,128)(2,1)S(1)}, u32[]{:S(2)}, u32[]{:S(2)}) collective-permute-start(bf16[3,32,128]{2,1,0:T(8,128)(2,1)S(1)} %pad_maximum_fusion.line_ref), channel_id=1, source_target_pairs={{0,1},{1,0},{2,3},{3,2},{4,5},{5,4},{6,7},{7,6},{8,9},{9,8},{10,11... | collective-permute-start | bytes 73736 | tf_op jit(solution)/shard_map/ppermute | solution.py:137
  9.0 3.3 %collective-permute-start.2 = (bf16[3,32,128]{2,1,0:T(8,128)(2,1)S(1)}, bf16[3,32,128]{2,1,0:T(8,128)(2,1)S(1)}, u32[]{:S(2)}, u32[]{:S(2)}) collective-permute-start(bf16[3,32,128]{2,1,0:T(8,128)(2,1)S(1)} %pad_maximum_fusion.line_ref), channel_id=1, source_target_pairs={{0,3},{1,2},{2,1},{3,0},{4,7},{5,6},{6,5},{7,4},{8,11},{9,10},{10,... | collective-permute-start | bytes 73736 | tf_op jit(solution)/shard_map/ppermute | solution.py:137
  10.7 1.6 %copy-start = (bf16[1024,1024]{1,0:T(8,128)(2,1)S(1)}, bf16[1024,1024]{1,0:T(8,128)(2,1)}, u32[]{:S(2)}) copy-start(bf16[1024,1024]{1,0:T(8,128)(2,1)} %mix_ref.1) | copy-start | bytes 6291460

commit v2 on v1

--- a/solution.py
+++ b/solution.py
@@ -10,8 +10,8 @@
 CELLS = BAND_LAT_CELLS * SECTOR_LON_CELLS
 BLOCK = 256
 INNER_TAPS = [(far, a, 1) for far in (0, 1) for a in range(3)]
-OUTER_TAPS = [(far, a, b) for far in (0, 1) for b in (0, 2) for a in range(3)]
-LON_SLOTS = (2, 0, 1)
+OUTER_TAPS = [(far, a, b) for b in (0, 2) for far in (0, 1) for a in range(3)]
+LON_SLOTS = (1, 0, 2)
 F32, BF16 = jnp.float32, jnp.bfloat16
 
 
@@ -60,7 +60,8 @@
         left_ref[:, p * wide : (p + 1) * wide] = jnp.where(low_half, first, second).astype(BF16)
 
 
-def inner_kernel(own_ref, line_ref, enc_ref, near_ref, far_ref, out_ref, taps_ref, left_ref):
+def inner_kernel(own_ref, line_ref, enc_ref, near_ref, far_ref, mix_ref, out_ref, taps_ref, left_ref):
+    del mix_ref
     features, channels = enc_ref.shape
     west, own, east = (doubled(line_ref[slot].astype(F32)) for slot in LON_SLOTS)
     store_pairs([*along_lon(west, own, east), west, own, east], left_ref)
@@ -91,33 +92,46 @@
     own_ref[...] = jnp.concatenate([high, sums - high], axis=1).astype(BF16)
 
 
-def mix_kernel(line_ref, odd_ref, even_ref, taps_ref, inner_ref, mix_ref, out_ref, *scratch):
-    left_ref, activ_ref, total_ref, state_ref, sems = scratch
+def other_band(line_ref, other_ref, taps_ref, left_ref, is_before, inside):
     wide = line_ref.shape[2]
     row = lax.broadcasted_iota(jnp.int32, (SECTOR_LON_CELLS, BAND_LAT_CELLS, wide), 1)
+    last = BAND_LAT_CELLS - 1
+    others, steps = [], []
+    for slot in LON_SLOTS:
+        own = doubled(line_ref[slot].astype(F32))
+        other = doubled(jnp.where(inside, other_ref[slot].astype(F32), 0.0))
+        down = jnp.where(row == 0, pltpu.roll(other, 1, 1), pltpu.roll(own, 1, 1))
+        up = jnp.where(row == last, pltpu.roll(other, last, 1), pltpu.roll(own, last, 1))
+        others.append(other)
+        steps.append(jnp.where(is_before, down, up))
+    store_pairs([*along_lon(*steps), *others], left_ref)
+    depth = taps_ref.shape[0] // 2
+    rows = pl.ds(pl.multiple_of(jnp.where(is_before, 0, depth), depth), depth)
+    for c in range(taps_ref.shape[1] // BLOCK):
+        cols = slice(c * BLOCK, (c + 1) * BLOCK)
+        yield cols, jnp.dot(left_ref[...], taps_ref[rows, cols], preferred_element_type=F32)
+
+
+def is_even():
+    return lax.rem(lax.axis_index("lat"), 2) == 0
+
+
+def pair_kernel(line_ref, other_ref, taps_ref, inner_ref, out_ref, left_ref):
+    for cols, added in other_band(line_ref, other_ref, taps_ref, left_ref, jnp.logical_not(is_even()), True):
+        out_ref[:, cols] = inner_ref[:, cols] + added
+
+
+def mix_kernel(line_ref, other_ref, taps_ref, inner_ref, mix_ref, out_ref, *scratch):
+    left_ref, activ_ref, total_ref, state_ref, sems = scratch
     band = lax.axis_index("lat")
-    even = lax.rem(band, 2) == 0
-    has_before, has_after = band > 0, band < lax.axis_size("lat") - 1
-    befores, afters, downs, ups = [], [], [], []
-    for slot in LON_SLOTS:
-        from_even, from_odd = even_ref[slot].astype(F32), odd_ref[slot].astype(F32)
-        before = doubled(jnp.where(has_before, jnp.where(even, from_odd, from_even), 0.0))
-        own = doubled(line_ref[slot].astype(F32))
-        after = doubled(jnp.where(has_after, jnp.where(even, from_even, from_odd), 0.0))
-        befores.append(before)
-        afters.append(after)
-        downs.append(jnp.where(row == 0, pltpu.roll(before, 1, 1), pltpu.roll(own, 1, 1)))
-        last = BAND_LAT_CELLS - 1
-        ups.append(jnp.where(row == last, pltpu.roll(after, last, 1), pltpu.roll(own, last, 1)))
-    store_pairs([*along_lon(*downs), *along_lon(*ups), *befores, *afters], left_ref)
-    channels = mix_ref.shape[0]
-    chunks = [slice(c * BLOCK, (c + 1) * BLOCK) for c in range(channels // BLOCK)]
-    for cols in chunks:
-        total = inner_ref[:, cols] + jnp.dot(left_ref[...], taps_ref[:, cols], preferred_element_type=F32)
+    inside = (band > 0) & (band < lax.axis_size("lat") - 1)
+    for cols, added in other_band(line_ref, other_ref, taps_ref, left_ref, is_even(), inside):
+        total = inner_ref[:, cols] + added
         activ_ref[:, cols] = jax.nn.gelu(total, approximate=True).astype(BF16)
         total_ref[:, cols] = total
     copies = []
-    for c, cols in enumerate(chunks):
+    for c in range(mix_ref.shape[1] // BLOCK):
+        cols = slice(c * BLOCK, (c + 1) * BLOCK)
         mixed = jnp.dot(activ_ref[...], mix_ref[:, cols], preferred_element_type=F32)
         state_ref[:, cols] = (total_ref[:, cols] + mixed).astype(BF16)
         copies.append(pltpu.make_async_copy(state_ref.at[:, cols], out_ref.at[:, cols], sems.at[c]))
@@ -168,7 +182,7 @@
         compiler_params=params,
         name="outer_taps",
     )(*weights)
-    line = jnp.stack([sent, from_neighbour(sent, "lon", 1), from_neighbour(sent, "lon", -1)])
+    line = jnp.stack([sent, from_neighbour(sent, "lon", -1), from_neighbour(sent, "lon", 1)])
     line, taps = lax.optimization_barrier((line, taps))
     inner = pl.pallas_call(
         inner_kernel,
@@ -177,14 +191,23 @@
         cost_estimate=pl.CostEstimate(flops=1_000_000_000, bytes_accessed=2_500_000, transcendentals=0),
         compiler_params=params,
         name="inner_taps",
-    )(own, line, *weights)
+    )(own, line, *weights, mix_weight)
+    left = pltpu.VMEM((CELLS, len(INNER_TAPS) * features), BF16)
+    paired = pl.pallas_call(
+        pair_kernel,
+        out_shape=pltpu.VMEM((CELLS, channels), F32),
+        scratch_shapes=[left],
+        cost_estimate=pl.CostEstimate(flops=1_000_000, bytes_accessed=10_000, transcendentals=0),
+        compiler_params=params,
+        name="pair_taps",
+    )(line, swapped(line, "lat", 0), taps, inner)
     mixed = pl.pallas_call(
         mix_kernel,
         out_shape=jax.ShapeDtypeStruct((CELLS, channels), BF16),
-        in_specs=[in_vmem] * 6,
+        in_specs=[in_vmem] * 5,
         out_specs=pl.BlockSpec(memory_space=pltpu.HBM),
         scratch_shapes=[
-            pltpu.VMEM((CELLS, len(OUTER_TAPS) * features), BF16),
+            left,
             pltpu.VMEM((CELLS, channels), BF16),
             pltpu.VMEM((CELLS, channels), F32),
             pltpu.VMEM((CELLS, channels), BF16),
@@ -192,7 +215,7 @@
         ],
         compiler_params=params,
         name="filter_and_mix",
-    )(line, swapped(line, "lat", 1), swapped(line, "lat", 0), taps, inner, mix_weight)
+    )(line, swapped(line, "lat", 1), taps, paired, mix_weight)
     return mixed.reshape(SECTOR_LON_CELLS, BAND_LAT_CELLS, channels)
 
 

time: 14.1 us -> 13.9 us (0.986)
  waiting for transfers between devices: 0.98 us -> 0.66 us
  Pallas kernels: 3.91 us -> 4.09 us
    ppermute x2, waiting for transfers between devices: 0.66 us -> 0.32 us  [swapped(): return lax.ppermute(value, axis, pairs)]
    pallas_call x0 -> x1, Pallas kernels: none -> 0.33 us  [on_device(): pl.pallas_call(pair_kernel, out_shape=pltpu.VMEM((CELLS, channels), F32),...]
  transfers between devices with their start and end apart: 4 -> 4, of which waited for: 2 -> 2; matrix products, arithmetic and copies ran while one was open for 0% -> 0% of each run, Pallas kernels for 15% -> 18%
where the time goes in v2:
time: 13.9 us; the launch traced here: 13.7 us
  starting transfers between devices  7.96 us (57%)
  Pallas kernels  4.09 us (29%)
  between operations  0.74 us (5%)
  waiting for transfers between devices  0.66 us (5%)
  local copies, waits for them, and re-layouts  0.25 us (2%)
    ppermute x2, starting transfers between devices, from_neighbour(): lax.ppermute(value, axis, [((i + step) % count, i) for i in range(count)])  6.12 us
    ppermute x2, starting transfers between devices, swapped(): return lax.ppermute(value, axis, pairs)  1.84 us
    pallas_call x1, Pallas kernels, on_device(): pl.pallas_call(mix_kernel, out_shape=jax.ShapeDtypeStruct((CELLS, channel...  1.41 us
    pallas_call x1, Pallas kernels, on_device(): pl.pallas_call(taps_kernel, out_shape=pltpu.VMEM((len(OUTER_TAPS) * featu...  1.21 us
    pallas_call x1, Pallas kernels, on_device(): pl.pallas_call(inner_kernel, out_shape=pltpu.VMEM((CELLS, channels), F32)...  0.89 us
    ppermute x2, waiting for transfers between devices, from_neighbour(): lax.ppermute(value, axis, [((i + step) % count, i) for i in range(count)])  0.34 us
    pallas_call x1, Pallas kernels, on_device(): pl.pallas_call(pair_kernel, out_shape=pltpu.VMEM((CELLS, channels), F32),...  0.33 us
    ppermute x2, waiting for transfers between devices, swapped(): return lax.ppermute(value, axis, pairs)  0.32 us
  transfers between devices with their start and end apart: 4, of which 2 were waited for; matrix products, arithmetic and copies ran while one was open for 0% of the time, Pallas kernels for 18%

profile of v2, /device:TPU:0, one launch (start us, length us, event | category | flops | bytes accessed | tf_op | source)
XLA Modules:
  0.0 13.7 jit_solution(5915487578913895465)
XLA Ops:
  0.0 0.0 copy-start.4
  0.0 0.0 copy-start.5
  0.7 0.2 %copy-done.4 = bf16[1,1,1024,64]{2,3,1,0:T(8,128)(2,1)S(1)} copy-done((bf16[1,1,1024,64]{2,3,1,0:T(8,128)(2,1)S(1)}, bf16[1,1,1024,64]{2,3,1,0:T(8,128)(2,1)}, u32[]{:S(2)}) %copy-start.4) | copy-done | bytes 131096
  0.9 0.0 copy-done.5
  0.9 0.0 copy-start.1
  0.9 0.0 copy-start.2
  0.9 0.0 copy-start.3
  0.9 0.2 %cell_sums.1 = (bf16[32,128]{1,0:T(8,128)(2,1)S(1)}, bf16[64,128]{1,0:T(8,128)(2,1)S(1)}) custom-call(f32[8,128]{1,0:T(8,128)S(1)} %ready.1._, s32[1,1]{1,0:T(1,128)S(6)} %copy.8.count_ref, bf16[64,1024]{1,0:T(8,128)(2,1)S(1)} %bitcast.9, s32[1,1024]{1,0:T(1,128)S(1)} %bitcast.10), custom_call_target="tpu_custom_call" | custom-call | flops 4000000000 | bytes 12000000 | tf_op jit(solution)/shard_map/cell_sums/pallas_call | solution.py:169
  1.2 0.0 copy-start
  1.2 3.0 %collective-permute-start = (bf16[32,128]{1,0:T(8,128)(2,1)S(1)}, bf16[32,128]{1,0:T(8,128)(2,1)S(1)}, u32[]{:S(2)}, u32[]{:S(2)}) collective-permute-start(bf16[32,128]{1,0:T(8,128)(2,1)S(1)} %get-tuple-element.13), channel_id=1, source_target_pairs={{28,0},{0,4},{4,8},{8,12},{12,16},{16,20},{20,24},{24,28},{29,1},{... | collective-permute-start | bytes 24584 | tf_op jit(solution)/shard_map/ppermute | solution.py:145
  4.2 3.1 %collective-permute-start.1 = (bf16[32,128]{1,0:T(8,128)(2,1)S(1)}, bf16[32,128]{1,0:T(8,128)(2,1)S(1)}, u32[]{:S(2)}, u32[]{:S(2)}) collective-permute-start(bf16[32,128]{1,0:T(8,128)(2,1)S(1)} %get-tuple-element.13), channel_id=1, source_target_pairs={{4,0},{8,4},{12,8},{16,12},{20,16},{24,20},{28,24},{0,28},{5,1},{9... | collective-permute-start | bytes 24584 | tf_op jit(solution)/shard_map/ppermute | solution.py:145
  7.3 0.0 copy-done.1
  7.3 0.0 copy-done.2
  7.3 0.0 copy-done.3
  7.3 1.2 %outer_taps.1.taps_ref = bf16[768,1024]{1,0:T(8,128)(2,1)S(1)} custom-call(bf16[64,1024]{1,0:T(8,128)(2,1)S(1)} %copy-done.3, bf16[3,3,64,1024]{3,2,1,0:T(8,128)(2,1)S(1)} %copy-done.1, bf16[3,3,64,1024]{3,2,1,0:T(8,128)(2,1)S(1)} %copy-done.2), custom_call_target="tpu_custom_call" | custom-call | flops 1600000000 | bytes 2500000 | tf_op jit(solution)/shard_map/outer_taps/pallas_call | solution.py:178
  8.6 0.3 %collective-permute-done = bf16[32,128]{1,0:T(8,128)(2,1)S(1)} collective-permute-done((bf16[32,128]{1,0:T(8,128)(2,1)S(1)}, bf16[32,128]{1,0:T(8,128)(2,1)S(1)}, u32[]{:S(2)}, u32[]{:S(2)}) %collective-permute-start) | collective-permute-done | bytes 8224 | tf_op jit(solution)/shard_map/ppermute | solution.py:145
  8.9 0.0 collective-permute-done.1
  8.9 0.1 collective-permute-start.3
  9.0 1.8 %collective-permute-start.2 = (bf16[3,32,128]{2,1,0:T(8,128)(2,1)S(1)}, bf16[3,32,128]{2,1,0:T(8,128)(2,1)S(1)}, u32[]{:S(2)}, u32[]{:S(2)}) collective-permute-start(bf16[3,32,128]{2,1,0:T(8,128)(2,1)S(1)} %pad_maximum_fusion.line_ref), channel_id=1, source_target_pairs={{0,3},{1,2},{2,1},{3,0},{4,7},{5,6},{6,5},{7,4},{8,11},{9,10},{10,... | collective-permute-start | bytes 73736 | tf_op jit(solution)/shard_map/ppermute | solution.py:151
  10.7 0.0 copy-done
  10.8 0.9 %inner_taps.1.inner_ref = f32[64,1024]{1,0:T(8,128)S(1)} custom-call(bf16[64,128]{1,0:T(8,128)(2,1)S(1)} %get-tuple-element.16.own_ref, bf16[3,32,128]{2,1,0:T(8,128)(2,1)S(1)} %pad_maximum_fusion.line_ref, bf16[64,1024]{1,0:T(8,128)(2,1)S(1)} %copy-done.3, bf16[3,3,64,1024]{3,2,1,0:T(8,128)(2,1)S(1)} %copy-done.1, bf16[3,3,64,1024]{3,2,1,0:T(8,128)(2,1)S(1)} %copy-done.2, ...), custom_call_target="tpu_custom_call" | custom-call | flops 1000000000 | bytes 2500000 | tf_op jit(solution)/shard_map/inner_taps/pallas_call | solution.py:187
  11.6 0.0 collective-permute-done.3.other_ref
  11.6 0.3 %pair_taps.1.inner_ref = f32[64,1024]{1,0:T(8,128)S(1)} custom-call(bf16[3,32,128]{2,1,0:T(8,128)(2,1)S(1)} %pad_maximum_fusion.line_ref, bf16[3,32,128]{2,1,0:T(8,128)(2,1)S(1)} %collective-permute-done.3.other_ref, bf16[768,1024]{1,0:T(8,128)(2,1)S(1)} %outer_taps.1.taps_ref, f32[64,1024]{1,0:T(8,128)S(1)} %inner_taps.1.inner_ref), custom_call_target="tpu_custom_call" | custom-call | flops 1000000 | bytes 10000 | tf_op jit(solution)/shard_map/pair_taps/pallas_call | solution.py:196
  12.0 0.3 %collective-permute-done.2.other_ref = bf16[3,32,128]{2,1,0:T(8,128)(2,1)S(1)} collective-permute-done((bf16[3,32,128]{2,1,0:T(8,128)(2,1)S(1)}, bf16[3,32,128]{2,1,0:T(8,128)(2,1)S(1)}, u32[]{:S(2)}, u32[]{:S(2)}) %collective-permute-start.2) | collective-permute-done | bytes 24608 | tf_op jit(solution)/shard_map/ppermute | solution.py:151
  12.3 1.4 %filter_and_mix.1 = bf16[64,1024]{1,0:T(8,128)(2,1)} custom-call(bf16[3,32,128]{2,1,0:T(8,128)(2,1)S(1)} %pad_maximum_fusion.line_ref, bf16[3,32,128]{2,1,0:T(8,128)(2,1)S(1)} %collective-permute-done.2.other_ref, bf16[768,1024]{1,0:T(8,128)(2,1)S(1)} %outer_taps.1.taps_ref, f32[64,1024]{1,0:T(8,128)S(1)} %pair_taps.1.inner_ref, bf16[1024,1024]{1,0:T(8,128)(2,1)S(1)} %copy-done), custom_call_target="tpu_custom_call" | custom-call | tf_op jit(solution)/shard_map/filter_and_mix/pallas_call | solution.py:204
  (2 shorter events, 0.0 us)
Async XLA Ops:
  0.0 0.9 %copy-start.4 = (bf16[1,1,1024,64]{2,3,1,0:T(8,128)(2,1)S(1)}, bf16[1,1,1024,64]{2,3,1,0:T(8,128)(2,1)}, u32[]{:S(2)}) copy-start(bf16[1,1,1024,64]{2,3,1,0:T(8,128)(2,1)} %param.7) | copy-start | bytes 393220
  0.0 0.9 %copy-start.5 = (s32[1,1,1024]{2,1,0:T(1,128)S(1)}, s32[1,1,1024]{2,1,0:T(1,128)}, u32[]{:S(2)}) copy-start(s32[1,1,1024]{2,1,0:T(1,128)} %param.8) | copy-start | bytes 12292
  0.9 6.4 %copy-start.1 = (bf16[3,3,64,1024]{3,2,1,0:T(8,128)(2,1)S(1)}, bf16[3,3,64,1024]{3,2,1,0:T(8,128)(2,1)}, u32[]{:S(2)}) copy-start(bf16[3,3,64,1024]{3,2,1,0:T(8,128)(2,1)} %near_ref.3) | copy-start | bytes 3538948
  0.9 6.4 %copy-start.2 = (bf16[3,3,64,1024]{3,2,1,0:T(8,128)(2,1)S(1)}, bf16[3,3,64,1024]{3,2,1,0:T(8,128)(2,1)}, u32[]{:S(2)}) copy-start(bf16[3,3,64,1024]{3,2,1,0:T(8,128)(2,1)} %far_ref.3) | copy-start | bytes 3538948
  0.9 6.4 %copy-start.3 = (bf16[64,1024]{1,0:T(8,128)(2,1)S(1)}, bf16[64,1024]{1,0:T(8,128)(2,1)}, u32[]{:S(2)}) copy-start(bf16[64,1024]{1,0:T(8,128)(2,1)} %enc_ref.3) | copy-start | bytes 393220
  1.2 9.6 %copy-start = (bf16[1024,1024]{1,0:T(8,128)(2,1)S(1)}, bf16[1024,1024]{1,0:T(8,128)(2,1)}, u32[]{:S(2)}) copy-start(bf16[1024,1024]{1,0:T(8,128)(2,1)} %mix_ref.3) | copy-start | bytes 6291460
  1.2 7.7 %collective-permute-start = (bf16[32,128]{1,0:T(8,128)(2,1)S(1)}, bf16[32,128]{1,0:T(8,128)(2,1)S(1)}, u32[]{:S(2)}, u32[]{:S(2)}) collective-permute-start(bf16[32,128]{1,0:T(8,128)(2,1)S(1)} %get-tuple-element.13), channel_id=1, source_target_pairs={{28,0},{0,4},{4,8},{8,12},{12,16},{16,20},{20,24},{24,28},{29,1},{... | collective-permute-start | bytes 24584 | tf_op jit(solution)/shard_map/ppermute | solution.py:145
  4.2 4.7 %collective-permute-start.1 = (bf16[32,128]{1,0:T(8,128)(2,1)S(1)}, bf16[32,128]{1,0:T(8,128)(2,1)S(1)}, u32[]{:S(2)}, u32[]{:S(2)}) collective-permute-start(bf16[32,128]{1,0:T(8,128)(2,1)S(1)} %get-tuple-element.13), channel_id=1, source_target_pairs={{4,0},{8,4},{12,8},{16,12},{20,16},{24,20},{28,24},{0,28},{5,1},{9... | collective-permute-start | bytes 24584 | tf_op jit(solution)/shard_map/ppermute | solution.py:145
  8.9 2.7 %collective-permute-start.3 = (bf16[3,32,128]{2,1,0:T(8,128)(2,1)S(1)}, bf16[3,32,128]{2,1,0:T(8,128)(2,1)S(1)}, u32[]{:S(2)}, u32[]{:S(2)}) collective-permute-start(bf16[3,32,128]{2,1,0:T(8,128)(2,1)S(1)} %pad_maximum_fusion.line_ref), channel_id=1, source_target_pairs={{0,1},{1,0},{2,3},{3,2},{4,5},{5,4},{6,7},{7,6},{8,9},{9,8},{10,11... | collective-permute-start | bytes 73736 | tf_op jit(solution)/shard_map/ppermute | solution.py:151
  9.0 3.3 %collective-permute-start.2 = (bf16[3,32,128]{2,1,0:T(8,128)(2,1)S(1)}, bf16[3,32,128]{2,1,0:T(8,128)(2,1)S(1)}, u32[]{:S(2)}, u32[]{:S(2)}) collective-permute-start(bf16[3,32,128]{2,1,0:T(8,128)(2,1)S(1)} %pad_maximum_fusion.line_ref), channel_id=1, source_target_pairs={{0,3},{1,2},{2,1},{3,0},{4,7},{5,6},{6,5},{7,4},{8,11},{9,10},{10,... | collective-permute-start | bytes 73736 | tf_op jit(solution)/shard_map/ppermute | solution.py:151

commit v3 on v2

--- a/solution.py
+++ b/solution.py
@@ -133,8 +133,8 @@
     for c in range(mix_ref.shape[1] // BLOCK):
         cols = slice(c * BLOCK, (c + 1) * BLOCK)
         mixed = jnp.dot(activ_ref[...], mix_ref[:, cols], preferred_element_type=F32)
-        state_ref[:, cols] = (total_ref[:, cols] + mixed).astype(BF16)
-        copies.append(pltpu.make_async_copy(state_ref.at[:, cols], out_ref.at[:, cols], sems.at[c]))
+        state_ref[c] = (total_ref[:, cols] + mixed).astype(BF16)
+        copies.append(pltpu.make_async_copy(state_ref.at[c], out_ref.at[:, cols], sems.at[c]))
         copies[-1].start()
     for copy in copies:
         copy.wait()
@@ -210,7 +210,7 @@
             left,
             pltpu.VMEM((CELLS, channels), BF16),
             pltpu.VMEM((CELLS, channels), F32),
-            pltpu.VMEM((CELLS, channels), BF16),
+            pltpu.VMEM((channels // BLOCK, CELLS, BLOCK), BF16),
             pltpu.SemaphoreType.DMA((channels // BLOCK,)),
         ],
         compiler_params=params,

time: 13.9 us -> 13.9 us (level)
  no operation moved by 1% of the time
where the time goes in v3:
time: 13.9 us; the launch traced here: 13.7 us
  starting transfers between devices  7.96 us (57%)
  Pallas kernels  4.09 us (29%)
  between operations  0.74 us (5%)
  waiting for transfers between devices  0.66 us (5%)
  local copies, waits for them, and re-layouts  0.25 us (2%)
    ppermute x2, starting transfers between devices, from_neighbour(): lax.ppermute(value, axis, [((i + step) % count, i) for i in range(count)])  6.12 us
    ppermute x2, starting transfers between devices, swapped(): return lax.ppermute(value, axis, pairs)  1.84 us
    pallas_call x1, Pallas kernels, on_device(): pl.pallas_call(mix_kernel, out_shape=jax.ShapeDtypeStruct((CELLS, channel...  1.41 us
    pallas_call x1, Pallas kernels, on_device(): pl.pallas_call(taps_kernel, out_shape=pltpu.VMEM((len(OUTER_TAPS) * featu...  1.21 us
    pallas_call x1, Pallas kernels, on_device(): pl.pallas_call(inner_kernel, out_shape=pltpu.VMEM((CELLS, channels), F32)...  0.89 us
    ppermute x2, waiting for transfers between devices, from_neighbour(): lax.ppermute(value, axis, [((i + step) % count, i) for i in range(count)])  0.34 us
    pallas_call x1, Pallas kernels, on_device(): pl.pallas_call(pair_kernel, out_shape=pltpu.VMEM((CELLS, channels), F32),...  0.33 us
    ppermute x2, waiting for transfers between devices, swapped(): return lax.ppermute(value, axis, pairs)  0.32 us
  transfers between devices with their start and end apart: 4, of which 2 were waited for; matrix products, arithmetic and copies ran while one was open for 0% of the time, Pallas kernels for 18%

profile of v3, /device:TPU:0, one launch (start us, length us, event | category | flops | bytes accessed | tf_op | source)
XLA Modules:
  0.0 13.7 jit_solution(6813769067966085080)
XLA Ops:
  0.0 0.0 copy-start.4
  0.0 0.0 copy-start.5
  0.7 0.2 %copy-done.4 = bf16[1,1,1024,64]{2,3,1,0:T(8,128)(2,1)S(1)} copy-done((bf16[1,1,1024,64]{2,3,1,0:T(8,128)(2,1)S(1)}, bf16[1,1,1024,64]{2,3,1,0:T(8,128)(2,1)}, u32[]{:S(2)}) %copy-start.4) | copy-done | bytes 131096
  0.9 0.0 copy-done.5
  0.9 0.0 copy-start.1
  0.9 0.0 copy-start.2
  0.9 0.0 copy-start.3
  0.9 0.2 %cell_sums.1 = (bf16[32,128]{1,0:T(8,128)(2,1)S(1)}, bf16[64,128]{1,0:T(8,128)(2,1)S(1)}) custom-call(f32[8,128]{1,0:T(8,128)S(1)} %ready.1._, s32[1,1]{1,0:T(1,128)S(6)} %copy.8.count_ref, bf16[64,1024]{1,0:T(8,128)(2,1)S(1)} %bitcast.9, s32[1,1024]{1,0:T(1,128)S(1)} %bitcast.10), custom_call_target="tpu_custom_call" | custom-call | flops 4000000000 | bytes 12000000 | tf_op jit(solution)/shard_map/cell_sums/pallas_call | solution.py:169
  1.2 0.0 copy-start
  1.2 3.0 %collective-permute-start = (bf16[32,128]{1,0:T(8,128)(2,1)S(1)}, bf16[32,128]{1,0:T(8,128)(2,1)S(1)}, u32[]{:S(2)}, u32[]{:S(2)}) collective-permute-start(bf16[32,128]{1,0:T(8,128)(2,1)S(1)} %get-tuple-element.13), channel_id=1, source_target_pairs={{28,0},{0,4},{4,8},{8,12},{12,16},{16,20},{20,24},{24,28},{29,1},{... | collective-permute-start | bytes 24584 | tf_op jit(solution)/shard_map/ppermute | solution.py:145
  4.2 3.1 %collective-permute-start.1 = (bf16[32,128]{1,0:T(8,128)(2,1)S(1)}, bf16[32,128]{1,0:T(8,128)(2,1)S(1)}, u32[]{:S(2)}, u32[]{:S(2)}) collective-permute-start(bf16[32,128]{1,0:T(8,128)(2,1)S(1)} %get-tuple-element.13), channel_id=1, source_target_pairs={{4,0},{8,4},{12,8},{16,12},{20,16},{24,20},{28,24},{0,28},{5,1},{9... | collective-permute-start | bytes 24584 | tf_op jit(solution)/shard_map/ppermute | solution.py:145
  7.3 0.0 copy-done.1
  7.3 0.0 copy-done.2
  7.3 0.0 copy-done.3
  7.3 1.2 %outer_taps.1.taps_ref = bf16[768,1024]{1,0:T(8,128)(2,1)S(1)} custom-call(bf16[64,1024]{1,0:T(8,128)(2,1)S(1)} %copy-done.3, bf16[3,3,64,1024]{3,2,1,0:T(8,128)(2,1)S(1)} %copy-done.1, bf16[3,3,64,1024]{3,2,1,0:T(8,128)(2,1)S(1)} %copy-done.2), custom_call_target="tpu_custom_call" | custom-call | flops 1600000000 | bytes 2500000 | tf_op jit(solution)/shard_map/outer_taps/pallas_call | solution.py:178
  8.6 0.3 %collective-permute-done = bf16[32,128]{1,0:T(8,128)(2,1)S(1)} collective-permute-done((bf16[32,128]{1,0:T(8,128)(2,1)S(1)}, bf16[32,128]{1,0:T(8,128)(2,1)S(1)}, u32[]{:S(2)}, u32[]{:S(2)}) %collective-permute-start) | collective-permute-done | bytes 8224 | tf_op jit(solution)/shard_map/ppermute | solution.py:145
  8.9 0.0 collective-permute-done.1
  8.9 0.1 collective-permute-start.3
  9.0 1.8 %collective-permute-start.2 = (bf16[3,32,128]{2,1,0:T(8,128)(2,1)S(1)}, bf16[3,32,128]{2,1,0:T(8,128)(2,1)S(1)}, u32[]{:S(2)}, u32[]{:S(2)}) collective-permute-start(bf16[3,32,128]{2,1,0:T(8,128)(2,1)S(1)} %pad_maximum_fusion.line_ref), channel_id=1, source_target_pairs={{0,3},{1,2},{2,1},{3,0},{4,7},{5,6},{6,5},{7,4},{8,11},{9,10},{10,... | collective-permute-start | bytes 73736 | tf_op jit(solution)/shard_map/ppermute | solution.py:151
  10.7 0.0 copy-done
  10.8 0.9 %inner_taps.1.inner_ref = f32[64,1024]{1,0:T(8,128)S(1)} custom-call(bf16[64,128]{1,0:T(8,128)(2,1)S(1)} %get-tuple-element.16.own_ref, bf16[3,32,128]{2,1,0:T(8,128)(2,1)S(1)} %pad_maximum_fusion.line_ref, bf16[64,1024]{1,0:T(8,128)(2,1)S(1)} %copy-done.3, bf16[3,3,64,1024]{3,2,1,0:T(8,128)(2,1)S(1)} %copy-done.1, bf16[3,3,64,1024]{3,2,1,0:T(8,128)(2,1)S(1)} %copy-done.2, ...), custom_call_target="tpu_custom_call" | custom-call | flops 1000000000 | bytes 2500000 | tf_op jit(solution)/shard_map/inner_taps/pallas_call | solution.py:187
  11.6 0.0 collective-permute-done.3.other_ref
  11.6 0.3 %pair_taps.1.inner_ref = f32[64,1024]{1,0:T(8,128)S(1)} custom-call(bf16[3,32,128]{2,1,0:T(8,128)(2,1)S(1)} %pad_maximum_fusion.line_ref, bf16[3,32,128]{2,1,0:T(8,128)(2,1)S(1)} %collective-permute-done.3.other_ref, bf16[768,1024]{1,0:T(8,128)(2,1)S(1)} %outer_taps.1.taps_ref, f32[64,1024]{1,0:T(8,128)S(1)} %inner_taps.1.inner_ref), custom_call_target="tpu_custom_call" | custom-call | flops 1000000 | bytes 10000 | tf_op jit(solution)/shard_map/pair_taps/pallas_call | solution.py:196
  12.0 0.3 %collective-permute-done.2.other_ref = bf16[3,32,128]{2,1,0:T(8,128)(2,1)S(1)} collective-permute-done((bf16[3,32,128]{2,1,0:T(8,128)(2,1)S(1)}, bf16[3,32,128]{2,1,0:T(8,128)(2,1)S(1)}, u32[]{:S(2)}, u32[]{:S(2)}) %collective-permute-start.2) | collective-permute-done | bytes 24608 | tf_op jit(solution)/shard_map/ppermute | solution.py:151
  12.3 1.4 %filter_and_mix.1 = bf16[64,1024]{1,0:T(8,128)(2,1)} custom-call(bf16[3,32,128]{2,1,0:T(8,128)(2,1)S(1)} %pad_maximum_fusion.line_ref, bf16[3,32,128]{2,1,0:T(8,128)(2,1)S(1)} %collective-permute-done.2.other_ref, bf16[768,1024]{1,0:T(8,128)(2,1)S(1)} %outer_taps.1.taps_ref, f32[64,1024]{1,0:T(8,128)S(1)} %pair_taps.1.inner_ref, bf16[1024,1024]{1,0:T(8,128)(2,1)S(1)} %copy-done), custom_call_target="tpu_custom_call" | custom-call | tf_op jit(solution)/shard_map/filter_and_mix/pallas_call | solution.py:204
  (2 shorter events, 0.0 us)
Async XLA Ops:
  0.0 0.9 %copy-start.4 = (bf16[1,1,1024,64]{2,3,1,0:T(8,128)(2,1)S(1)}, bf16[1,1,1024,64]{2,3,1,0:T(8,128)(2,1)}, u32[]{:S(2)}) copy-start(bf16[1,1,1024,64]{2,3,1,0:T(8,128)(2,1)} %param.7) | copy-start | bytes 393220
  0.0 0.9 %copy-start.5 = (s32[1,1,1024]{2,1,0:T(1,128)S(1)}, s32[1,1,1024]{2,1,0:T(1,128)}, u32[]{:S(2)}) copy-start(s32[1,1,1024]{2,1,0:T(1,128)} %param.8) | copy-start | bytes 12292
  0.9 6.4 %copy-start.1 = (bf16[3,3,64,1024]{3,2,1,0:T(8,128)(2,1)S(1)}, bf16[3,3,64,1024]{3,2,1,0:T(8,128)(2,1)}, u32[]{:S(2)}) copy-start(bf16[3,3,64,1024]{3,2,1,0:T(8,128)(2,1)} %near_ref.3) | copy-start | bytes 3538948
  0.9 6.4 %copy-start.2 = (bf16[3,3,64,1024]{3,2,1,0:T(8,128)(2,1)S(1)}, bf16[3,3,64,1024]{3,2,1,0:T(8,128)(2,1)}, u32[]{:S(2)}) copy-start(bf16[3,3,64,1024]{3,2,1,0:T(8,128)(2,1)} %far_ref.3) | copy-start | bytes 3538948
  0.9 6.4 %copy-start.3 = (bf16[64,1024]{1,0:T(8,128)(2,1)S(1)}, bf16[64,1024]{1,0:T(8,128)(2,1)}, u32[]{:S(2)}) copy-start(bf16[64,1024]{1,0:T(8,128)(2,1)} %enc_ref.3) | copy-start | bytes 393220
  1.2 9.6 %copy-start = (bf16[1024,1024]{1,0:T(8,128)(2,1)S(1)}, bf16[1024,1024]{1,0:T(8,128)(2,1)}, u32[]{:S(2)}) copy-start(bf16[1024,1024]{1,0:T(8,128)(2,1)} %mix_ref.3) | copy-start | bytes 6291460
  1.2 7.7 %collective-permute-start = (bf16[32,128]{1,0:T(8,128)(2,1)S(1)}, bf16[32,128]{1,0:T(8,128)(2,1)S(1)}, u32[]{:S(2)}, u32[]{:S(2)}) collective-permute-start(bf16[32,128]{1,0:T(8,128)(2,1)S(1)} %get-tuple-element.13), channel_id=1, source_target_pairs={{28,0},{0,4},{4,8},{8,12},{12,16},{16,20},{20,24},{24,28},{29,1},{... | collective-permute-start | bytes 24584 | tf_op jit(solution)/shard_map/ppermute | solution.py:145
  4.2 4.7 %collective-permute-start.1 = (bf16[32,128]{1,0:T(8,128)(2,1)S(1)}, bf16[32,128]{1,0:T(8,128)(2,1)S(1)}, u32[]{:S(2)}, u32[]{:S(2)}) collective-permute-start(bf16[32,128]{1,0:T(8,128)(2,1)S(1)} %get-tuple-element.13), channel_id=1, source_target_pairs={{4,0},{8,4},{12,8},{16,12},{20,16},{24,20},{28,24},{0,28},{5,1},{9... | collective-permute-start | bytes 24584 | tf_op jit(solution)/shard_map/ppermute | solution.py:145
  8.9 2.7 %collective-permute-start.3 = (bf16[3,32,128]{2,1,0:T(8,128)(2,1)S(1)}, bf16[3,32,128]{2,1,0:T(8,128)(2,1)S(1)}, u32[]{:S(2)}, u32[]{:S(2)}) collective-permute-start(bf16[3,32,128]{2,1,0:T(8,128)(2,1)S(1)} %pad_maximum_fusion.line_ref), channel_id=1, source_target_pairs={{0,1},{1,0},{2,3},{3,2},{4,5},{5,4},{6,7},{7,6},{8,9},{9,8},{10,11... | collective-permute-start | bytes 73736 | tf_op jit(solution)/shard_map/ppermute | solution.py:151
  9.0 3.3 %collective-permute-start.2 = (bf16[3,32,128]{2,1,0:T(8,128)(2,1)S(1)}, bf16[3,32,128]{2,1,0:T(8,128)(2,1)S(1)}, u32[]{:S(2)}, u32[]{:S(2)}) collective-permute-start(bf16[3,32,128]{2,1,0:T(8,128)(2,1)S(1)} %pad_maximum_fusion.line_ref), channel_id=1, source_target_pairs={{0,3},{1,2},{2,1},{3,0},{4,7},{5,6},{6,5},{7,4},{8,11},{9,10},{10,... | collective-permute-start | bytes 73736 | tf_op jit(solution)/shard_map/ppermute | solution.py:151

commit v4 on v2

--- a/solution.py
+++ b/solution.py
@@ -107,8 +107,8 @@
     store_pairs([*along_lon(*steps), *others], left_ref)
     depth = taps_ref.shape[0] // 2
     rows = pl.ds(pl.multiple_of(jnp.where(is_before, 0, depth), depth), depth)
-    for c in range(taps_ref.shape[1] // BLOCK):
-        cols = slice(c * BLOCK, (c + 1) * BLOCK)
+    for c in range(taps_ref.shape[1] // (2 * BLOCK)):
+        cols = slice(2 * c * BLOCK, 2 * (c + 1) * BLOCK)
         yield cols, jnp.dot(left_ref[...], taps_ref[rows, cols], preferred_element_type=F32)
 
 

time: 13.9 us -> 13.9 us (level)
  no operation moved by 1% of the time
where the time goes in v4:
time: 13.9 us; the launch traced here: 13.7 us
  starting transfers between devices  7.96 us (57%)
  Pallas kernels  4.09 us (29%)
  between operations  0.74 us (5%)
  waiting for transfers between devices  0.66 us (5%)
  local copies, waits for them, and re-layouts  0.25 us (2%)
    ppermute x2, starting transfers between devices, from_neighbour(): lax.ppermute(value, axis, [((i + step) % count, i) for i in range(count)])  6.12 us
    ppermute x2, starting transfers between devices, swapped(): return lax.ppermute(value, axis, pairs)  1.84 us
    pallas_call x1, Pallas kernels, on_device(): pl.pallas_call(mix_kernel, out_shape=jax.ShapeDtypeStruct((CELLS, channel...  1.41 us
    pallas_call x1, Pallas kernels, on_device(): pl.pallas_call(taps_kernel, out_shape=pltpu.VMEM((len(OUTER_TAPS) * featu...  1.21 us
    pallas_call x1, Pallas kernels, on_device(): pl.pallas_call(inner_kernel, out_shape=pltpu.VMEM((CELLS, channels), F32)...  0.89 us
    ppermute x2, waiting for transfers between devices, from_neighbour(): lax.ppermute(value, axis, [((i + step) % count, i) for i in range(count)])  0.34 us
    pallas_call x1, Pallas kernels, on_device(): pl.pallas_call(pair_kernel, out_shape=pltpu.VMEM((CELLS, channels), F32),...  0.33 us
    ppermute x2, waiting for transfers between devices, swapped(): return lax.ppermute(value, axis, pairs)  0.32 us
  transfers between devices with their start and end apart: 4, of which 2 were waited for; matrix products, arithmetic and copies ran while one was open for 0% of the time, Pallas kernels for 18%

profile of v4, /device:TPU:0, one launch (start us, length us, event | category | flops | bytes accessed | tf_op | source)
XLA Modules:
  0.0 13.7 jit_solution(5915487578913895465)
XLA Ops:
  0.0 0.0 copy-start.4
  0.0 0.0 copy-start.5
  0.7 0.2 %copy-done.4 = bf16[1,1,1024,64]{2,3,1,0:T(8,128)(2,1)S(1)} copy-done((bf16[1,1,1024,64]{2,3,1,0:T(8,128)(2,1)S(1)}, bf16[1,1,1024,64]{2,3,1,0:T(8,128)(2,1)}, u32[]{:S(2)}) %copy-start.4) | copy-done | bytes 131096
  0.9 0.0 copy-done.5
  0.9 0.0 copy-start.1
  0.9 0.0 copy-start.2
  0.9 0.0 copy-start.3
  0.9 0.2 %cell_sums.1 = (bf16[32,128]{1,0:T(8,128)(2,1)S(1)}, bf16[64,128]{1,0:T(8,128)(2,1)S(1)}) custom-call(f32[8,128]{1,0:T(8,128)S(1)} %ready.1._, s32[1,1]{1,0:T(1,128)S(6)} %copy.8.count_ref, bf16[64,1024]{1,0:T(8,128)(2,1)S(1)} %bitcast.9, s32[1,1024]{1,0:T(1,128)S(1)} %bitcast.10), custom_call_target="tpu_custom_call" | custom-call | flops 4000000000 | bytes 12000000 | tf_op jit(solution)/shard_map/cell_sums/pallas_call | solution.py:169
  1.2 0.0 copy-start
  1.2 3.0 %collective-permute-start = (bf16[32,128]{1,0:T(8,128)(2,1)S(1)}, bf16[32,128]{1,0:T(8,128)(2,1)S(1)}, u32[]{:S(2)}, u32[]{:S(2)}) collective-permute-start(bf16[32,128]{1,0:T(8,128)(2,1)S(1)} %get-tuple-element.13), channel_id=1, source_target_pairs={{28,0},{0,4},{4,8},{8,12},{12,16},{16,20},{20,24},{24,28},{29,1},{... | collective-permute-start | bytes 24584 | tf_op jit(solution)/shard_map/ppermute | solution.py:145
  4.2 3.1 %collective-permute-start.1 = (bf16[32,128]{1,0:T(8,128)(2,1)S(1)}, bf16[32,128]{1,0:T(8,128)(2,1)S(1)}, u32[]{:S(2)}, u32[]{:S(2)}) collective-permute-start(bf16[32,128]{1,0:T(8,128)(2,1)S(1)} %get-tuple-element.13), channel_id=1, source_target_pairs={{4,0},{8,4},{12,8},{16,12},{20,16},{24,20},{28,24},{0,28},{5,1},{9... | collective-permute-start | bytes 24584 | tf_op jit(solution)/shard_map/ppermute | solution.py:145
  7.3 0.0 copy-done.1
  7.3 0.0 copy-done.2
  7.3 0.0 copy-done.3
  7.3 1.2 %outer_taps.1.taps_ref = bf16[768,1024]{1,0:T(8,128)(2,1)S(1)} custom-call(bf16[64,1024]{1,0:T(8,128)(2,1)S(1)} %copy-done.3, bf16[3,3,64,1024]{3,2,1,0:T(8,128)(2,1)S(1)} %copy-done.1, bf16[3,3,64,1024]{3,2,1,0:T(8,128)(2,1)S(1)} %copy-done.2), custom_call_target="tpu_custom_call" | custom-call | flops 1600000000 | bytes 2500000 | tf_op jit(solution)/shard_map/outer_taps/pallas_call | solution.py:178
  8.6 0.3 %collective-permute-done = bf16[32,128]{1,0:T(8,128)(2,1)S(1)} collective-permute-done((bf16[32,128]{1,0:T(8,128)(2,1)S(1)}, bf16[32,128]{1,0:T(8,128)(2,1)S(1)}, u32[]{:S(2)}, u32[]{:S(2)}) %collective-permute-start) | collective-permute-done | bytes 8224 | tf_op jit(solution)/shard_map/ppermute | solution.py:145
  8.9 0.0 collective-permute-done.1
  8.9 0.1 collective-permute-start.3
  9.0 1.8 %collective-permute-start.2 = (bf16[3,32,128]{2,1,0:T(8,128)(2,1)S(1)}, bf16[3,32,128]{2,1,0:T(8,128)(2,1)S(1)}, u32[]{:S(2)}, u32[]{:S(2)}) collective-permute-start(bf16[3,32,128]{2,1,0:T(8,128)(2,1)S(1)} %pad_maximum_fusion.line_ref), channel_id=1, source_target_pairs={{0,3},{1,2},{2,1},{3,0},{4,7},{5,6},{6,5},{7,4},{8,11},{9,10},{10,... | collective-permute-start | bytes 73736 | tf_op jit(solution)/shard_map/ppermute | solution.py:151
  10.7 0.0 copy-done
  10.8 0.9 %inner_taps.1.inner_ref = f32[64,1024]{1,0:T(8,128)S(1)} custom-call(bf16[64,128]{1,0:T(8,128)(2,1)S(1)} %get-tuple-element.16.own_ref, bf16[3,32,128]{2,1,0:T(8,128)(2,1)S(1)} %pad_maximum_fusion.line_ref, bf16[64,1024]{1,0:T(8,128)(2,1)S(1)} %copy-done.3, bf16[3,3,64,1024]{3,2,1,0:T(8,128)(2,1)S(1)} %copy-done.1, bf16[3,3,64,1024]{3,2,1,0:T(8,128)(2,1)S(1)} %copy-done.2, ...), custom_call_target="tpu_custom_call" | custom-call | flops 1000000000 | bytes 2500000 | tf_op jit(solution)/shard_map/inner_taps/pallas_call | solution.py:187
  11.6 0.0 collective-permute-done.3.other_ref
  11.6 0.3 %pair_taps.1.inner_ref = f32[64,1024]{1,0:T(8,128)S(1)} custom-call(bf16[3,32,128]{2,1,0:T(8,128)(2,1)S(1)} %pad_maximum_fusion.line_ref, bf16[3,32,128]{2,1,0:T(8,128)(2,1)S(1)} %collective-permute-done.3.other_ref, bf16[768,1024]{1,0:T(8,128)(2,1)S(1)} %outer_taps.1.taps_ref, f32[64,1024]{1,0:T(8,128)S(1)} %inner_taps.1.inner_ref), custom_call_target="tpu_custom_call" | custom-call | flops 1000000 | bytes 10000 | tf_op jit(solution)/shard_map/pair_taps/pallas_call | solution.py:196
  12.0 0.3 %collective-permute-done.2.other_ref = bf16[3,32,128]{2,1,0:T(8,128)(2,1)S(1)} collective-permute-done((bf16[3,32,128]{2,1,0:T(8,128)(2,1)S(1)}, bf16[3,32,128]{2,1,0:T(8,128)(2,1)S(1)}, u32[]{:S(2)}, u32[]{:S(2)}) %collective-permute-start.2) | collective-permute-done | bytes 24608 | tf_op jit(solution)/shard_map/ppermute | solution.py:151
  12.3 1.4 %filter_and_mix.1 = bf16[64,1024]{1,0:T(8,128)(2,1)} custom-call(bf16[3,32,128]{2,1,0:T(8,128)(2,1)S(1)} %pad_maximum_fusion.line_ref, bf16[3,32,128]{2,1,0:T(8,128)(2,1)S(1)} %collective-permute-done.2.other_ref, bf16[768,1024]{1,0:T(8,128)(2,1)S(1)} %outer_taps.1.taps_ref, f32[64,1024]{1,0:T(8,128)S(1)} %pair_taps.1.inner_ref, bf16[1024,1024]{1,0:T(8,128)(2,1)S(1)} %copy-done), custom_call_target="tpu_custom_call" | custom-call | tf_op jit(solution)/shard_map/filter_and_mix/pallas_call | solution.py:204
  (2 shorter events, 0.0 us)
Async XLA Ops:
  0.0 0.9 %copy-start.4 = (bf16[1,1,1024,64]{2,3,1,0:T(8,128)(2,1)S(1)}, bf16[1,1,1024,64]{2,3,1,0:T(8,128)(2,1)}, u32[]{:S(2)}) copy-start(bf16[1,1,1024,64]{2,3,1,0:T(8,128)(2,1)} %param.7) | copy-start | bytes 393220
  0.0 0.9 %copy-start.5 = (s32[1,1,1024]{2,1,0:T(1,128)S(1)}, s32[1,1,1024]{2,1,0:T(1,128)}, u32[]{:S(2)}) copy-start(s32[1,1,1024]{2,1,0:T(1,128)} %param.8) | copy-start | bytes 12292
  0.9 6.4 %copy-start.1 = (bf16[3,3,64,1024]{3,2,1,0:T(8,128)(2,1)S(1)}, bf16[3,3,64,1024]{3,2,1,0:T(8,128)(2,1)}, u32[]{:S(2)}) copy-start(bf16[3,3,64,1024]{3,2,1,0:T(8,128)(2,1)} %near_ref.3) | copy-start | bytes 3538948
  0.9 6.4 %copy-start.2 = (bf16[3,3,64,1024]{3,2,1,0:T(8,128)(2,1)S(1)}, bf16[3,3,64,1024]{3,2,1,0:T(8,128)(2,1)}, u32[]{:S(2)}) copy-start(bf16[3,3,64,1024]{3,2,1,0:T(8,128)(2,1)} %far_ref.3) | copy-start | bytes 3538948
  0.9 6.4 %copy-start.3 = (bf16[64,1024]{1,0:T(8,128)(2,1)S(1)}, bf16[64,1024]{1,0:T(8,128)(2,1)}, u32[]{:S(2)}) copy-start(bf16[64,1024]{1,0:T(8,128)(2,1)} %enc_ref.3) | copy-start | bytes 393220
  1.2 9.6 %copy-start = (bf16[1024,1024]{1,0:T(8,128)(2,1)S(1)}, bf16[1024,1024]{1,0:T(8,128)(2,1)}, u32[]{:S(2)}) copy-start(bf16[1024,1024]{1,0:T(8,128)(2,1)} %mix_ref.3) | copy-start | bytes 6291460
  1.2 7.7 %collective-permute-start = (bf16[32,128]{1,0:T(8,128)(2,1)S(1)}, bf16[32,128]{1,0:T(8,128)(2,1)S(1)}, u32[]{:S(2)}, u32[]{:S(2)}) collective-permute-start(bf16[32,128]{1,0:T(8,128)(2,1)S(1)} %get-tuple-element.13), channel_id=1, source_target_pairs={{28,0},{0,4},{4,8},{8,12},{12,16},{16,20},{20,24},{24,28},{29,1},{... | collective-permute-start | bytes 24584 | tf_op jit(solution)/shard_map/ppermute | solution.py:145
  4.2 4.7 %collective-permute-start.1 = (bf16[32,128]{1,0:T(8,128)(2,1)S(1)}, bf16[32,128]{1,0:T(8,128)(2,1)S(1)}, u32[]{:S(2)}, u32[]{:S(2)}) collective-permute-start(bf16[32,128]{1,0:T(8,128)(2,1)S(1)} %get-tuple-element.13), channel_id=1, source_target_pairs={{4,0},{8,4},{12,8},{16,12},{20,16},{24,20},{28,24},{0,28},{5,1},{9... | collective-permute-start | bytes 24584 | tf_op jit(solution)/shard_map/ppermute | solution.py:145
  8.9 2.7 %collective-permute-start.3 = (bf16[3,32,128]{2,1,0:T(8,128)(2,1)S(1)}, bf16[3,32,128]{2,1,0:T(8,128)(2,1)S(1)}, u32[]{:S(2)}, u32[]{:S(2)}) collective-permute-start(bf16[3,32,128]{2,1,0:T(8,128)(2,1)S(1)} %pad_maximum_fusion.line_ref), channel_id=1, source_target_pairs={{0,1},{1,0},{2,3},{3,2},{4,5},{5,4},{6,7},{7,6},{8,9},{9,8},{10,11... | collective-permute-start | bytes 73736 | tf_op jit(solution)/shard_map/ppermute | solution.py:151
  9.0 3.3 %collective-permute-start.2 = (bf16[3,32,128]{2,1,0:T(8,128)(2,1)S(1)}, bf16[3,32,128]{2,1,0:T(8,128)(2,1)S(1)}, u32[]{:S(2)}, u32[]{:S(2)}) collective-permute-start(bf16[3,32,128]{2,1,0:T(8,128)(2,1)S(1)} %pad_maximum_fusion.line_ref), channel_id=1, source_target_pairs={{0,3},{1,2},{2,1},{3,0},{4,7},{5,6},{6,5},{7,4},{8,11},{9,10},{10,... | collective-permute-start | bytes 73736 | tf_op jit(solution)/shard_map/ppermute | solution.py:151
